TPU v7x, 256 devices: a whole 4x4x8 slice. The times are simulated.
256 devices in a mesh: head: 8 (over x, y_hi), tok: 32 (over y_lo, z, core).
Axes of the slice: x: 4, y: 4 (y_hi: 2, y_lo: 2; y = y_hi * 2 + y_lo), z: 8, core: 2. Of those that a mesh axis runs over, the one named last changes fastest.
Arguments:
- anchors: bfloat16 [4096, 1024], P('tok'), may hold values from -26 to 26
- cells: bfloat16 [16384, 1024], P('tok'), may hold values from -26 to 26
- w_query: bfloat16 [1024, 1024], P(None, 'head'), may hold values from -0.125 to 0.125
- w_key: bfloat16 [1024, 1024], P(None, 'head'), may hold values from -0.15625 to 0.15625
- w_value: bfloat16 [1024, 1024], P(None, 'head'), may hold values from -0.1875 to 0.1875
- w_out: bfloat16 [1024, 1024], P('head'), may hold values from -0.1875 to 0.1875
- grad_out_anchors: bfloat16 [4096, 1024], P('tok'), may hold values from -96 to 96
- grad_out_cells: bfloat16 [16384, 1024], P('tok'), may hold values from -96 to 96
Outputs:
- grad_anchors: bfloat16 [4096, 1024], P('tok', 'head')
- grad_cells: bfloat16 [16384, 1024], P('tok', 'head')
All inputs are finite; a program needn't handle non-finite values.
Results may differ from a plain program's by a relative error of at most 0.035.
Values may be sent and summed in bfloat16 or wider, within the bound.
No kernel may reach another device: no remote copies, remote signals or barrier semaphores. Data moves between devices by JAX's collectives and lax.ppermute only.
A program may use at most 64 MiB of HBM per device.

v0:
```python
from functools import partial
import math

import jax
import jax.numpy as jnp
from jax import lax
from jax.sharding import PartitionSpec as P

HEAD_DIM = 64


def block_width(total_keys):
    return math.gcd(total_keys, 512)


def split_heads(matrix):
    return matrix.reshape(matrix.shape[0], -1, HEAD_DIM)


def project_back(gradient, weight):
    return lax.dot_general(
        gradient, weight, (((1,), (1,)), ((), ())), preferred_element_type=jnp.float32
    )


def over_blocks(advance, carried, key_rows, value_rows):
    total_keys = key_rows.shape[0]
    width_now = block_width(total_keys)

    def one_block(block_index, carried_now):
        offset = block_index * width_now
        key_part = lax.dynamic_slice_in_dim(key_rows, offset, width_now, 0)
        value_part = lax.dynamic_slice_in_dim(value_rows, offset, width_now, 0)
        return advance(carried_now, key_part, value_part, offset)

    return lax.fori_loop(0, total_keys // width_now, one_block, carried)


def forward_block(carried, key_part, value_part, key_offset, queries):
    run_peak, run_total, run_sum = carried
    scores = jnp.einsum(
        "rhc,khc->hrk", queries, split_heads(key_part), preferred_element_type=jnp.float32
    ) * HEAD_DIM ** (-0.5)
    new_peak = jnp.maximum(run_peak, jnp.max(scores, axis=2))
    factor = jnp.exp(run_peak - new_peak)
    weights = jnp.exp(scores - new_peak[:, :, None])
    run_total = run_total * factor + jnp.sum(weights, axis=2)
    run_sum = run_sum * factor[:, :, None] + jnp.einsum(
        "hrk,khc->hrc",
        weights.astype(jnp.bfloat16),
        split_heads(value_part),
        preferred_element_type=jnp.float32,
    )
    return (new_peak, run_total, run_sum)


def score_terms(key_part, value_part, queries, grad_heads, log_total, delta_rows):
    key_heads = split_heads(key_part)
    value_heads = split_heads(value_part)
    scores = jnp.einsum(
        "rhc,khc->hrk", queries, key_heads, preferred_element_type=jnp.float32
    ) * HEAD_DIM ** (-0.5)
    weights = jnp.exp(scores - log_total[:, :, None])
    weights_low = weights.astype(jnp.bfloat16)
    dprobs = jnp.einsum("rhc,khc->hrk", grad_heads, value_heads, preferred_element_type=jnp.float32)
    dscore = (weights * (dprobs - delta_rows[:, :, None])).astype(jnp.bfloat16)
    return (key_heads, weights_low, dscore)


def pair_piece(weights_low, dscore, queries, grad_heads):
    key_piece = jnp.einsum(
        "hrk,rhc->khc", dscore, queries, preferred_element_type=jnp.float32
    ) * HEAD_DIM ** (-0.5)
    value_piece = jnp.einsum(
        "hrk,rhc->khc", weights_low, grad_heads, preferred_element_type=jnp.float32
    )
    return jnp.concatenate(
        [key_piece.reshape(key_piece.shape[0], -1), value_piece.reshape(value_piece.shape[0], -1)],
        axis=1,
    )


def backward_block(
    carried,
    key_part,
    value_part,
    key_offset,
    queries,
    grad_heads,
    log_total,
    delta_rows,
    with_pairs,
):
    key_heads, weights_low, dscore = score_terms(
        key_part, value_part, queries, grad_heads, log_total, delta_rows
    )
    grad_query = carried[0] + jnp.einsum(
        "hrk,khc->rhc", dscore, key_heads, preferred_element_type=jnp.float32
    )
    fresh_piece = pair_piece(weights_low, dscore, queries, grad_heads)
    return (grad_query, lax.dynamic_update_slice_in_dim(carried[1], fresh_piece, key_offset, 0))


def per_device(anchors, cells, w_query, w_key, w_value, w_out, grad_out_anchors, grad_out_cells):
    anchor_count = anchors.shape[0]
    row_total = anchor_count + cells.shape[0]
    channels = w_query.shape[1]
    heads_here = channels // HEAD_DIM
    key_total = anchor_count * lax.axis_size("tok")
    row_data = jnp.concatenate([anchors, cells], axis=0)
    cotangent = jnp.concatenate([grad_out_anchors, grad_out_cells], axis=0)
    queries = split_heads(
        jnp.dot(row_data, w_query, preferred_element_type=jnp.float32).astype(jnp.bfloat16)
    )
    key_local = jnp.dot(anchors, w_key, preferred_element_type=jnp.float32).astype(jnp.bfloat16)
    value_local = jnp.dot(anchors, w_value, preferred_element_type=jnp.float32).astype(jnp.bfloat16)
    grad_heads = split_heads(project_back(cotangent, w_out).astype(jnp.bfloat16))
    start_forward = (
        jnp.full((heads_here, row_total), -1e30, jnp.float32),
        jnp.zeros((heads_here, row_total), jnp.float32),
        jnp.zeros((heads_here, row_total, HEAD_DIM), jnp.float32),
    )
    query_zeros = jnp.zeros((row_total, heads_here, HEAD_DIM), jnp.float32)
    forward_step = partial(forward_block, queries=queries)
    start_backward = (query_zeros, jnp.zeros((key_total, 2 * channels), jnp.float32))
    shard_pair = (
        lax.all_gather(key_local, "tok", axis=0, tiled=True),
        lax.all_gather(value_local, "tok", axis=0, tiled=True),
    )
    run_peak, run_total, run_sum = over_blocks(
        forward_step, start_forward, shard_pair[0], shard_pair[1]
    )
    log_total = run_peak + jnp.log(run_total)
    outputs = run_sum / run_total[:, :, None]
    delta_rows = jnp.sum(jnp.transpose(grad_heads, (1, 0, 2)).astype(jnp.float32) * outputs, axis=2)
    log_total, delta_rows = (log_total, delta_rows)
    backward_step = partial(
        backward_block,
        queries=queries,
        grad_heads=grad_heads,
        log_total=log_total,
        delta_rows=delta_rows,
        with_pairs=True,
    )
    shard_pair = (
        lax.all_gather(key_local, "tok", axis=0, tiled=True),
        lax.all_gather(value_local, "tok", axis=0, tiled=True),
    )
    finished = over_blocks(backward_step, start_backward, shard_pair[0], shard_pair[1])
    grad_query = (
        (finished[0] * HEAD_DIM ** (-0.5)).astype(jnp.bfloat16).reshape(row_total, channels)
    )
    cell_part = project_back(grad_query[anchor_count:], w_query)
    combined = lax.psum_scatter(
        finished[1].astype(jnp.bfloat16), "tok", scatter_dimension=0, tiled=True
    ).astype(jnp.float32)
    key_grad = combined[:, :channels].astype(jnp.bfloat16)
    value_grad = combined[:, channels:].astype(jnp.bfloat16)
    anchor_part = (
        project_back(grad_query[:anchor_count], w_query)
        + project_back(key_grad, w_key)
        + project_back(value_grad, w_value)
    )
    anchor_grad, cell_grad = (
        lax.psum_scatter(
            anchor_part.astype(jnp.bfloat16), "head", scatter_dimension=1, tiled=True
        ).astype(jnp.float32),
        lax.psum_scatter(
            cell_part.astype(jnp.bfloat16), "head", scatter_dimension=1, tiled=True
        ).astype(jnp.float32),
    )
    return (anchor_grad.astype(jnp.bfloat16), cell_grad.astype(jnp.bfloat16))


def solution(mesh):
    return jax.shard_map(
        per_device,
        mesh=mesh,
        in_specs=(
            P("tok", None),
            P("tok", None),
            P(None, "head"),
            P(None, "head"),
            P(None, "head"),
            P("head", None),
            P("tok", None),
            P("tok", None),
        ),
        out_specs=(P("tok", "head"), P("tok", "head")),
        check_vma=False,
    )
```

profile of v0, /device:TPU:6, one launch (start us, length us, event | category | flops | bytes accessed | tf_op | source)
XLA Modules:
  0.0 500.9 jit_solution(2389482854932158343)
XLA Ops:
  7.3 2.0 convolution_convert_fusion.1
  9.3 1.9 convolution_convert_fusion.2
  11.3 1.8 fusion.32
  13.7 63.3 %all-gather.5.cloned.1.call-done = bf16[4096,128]{1,0:T(8,128)(2,1)} async-done(((bf16[128,128]{1,0:T(8,128)(2,1)}), bf16[4096,128]{1,0:T(8,128)(2,1)}) %all-gather.5.cloned.1.call-update) | async-done | bytes 1048592 | tf_op jit(solution)/shard_map/all_gather | solution.py:147
  77.0 2.3 copy.17
  79.3 63.4 %all-gather.3.cloned.1.call-done = bf16[4096,128]{1,0:T(8,128)(2,1)} async-done(((bf16[128,128]{1,0:T(8,128)(2,1)}), bf16[4096,128]{1,0:T(8,128)(2,1)}) %all-gather.3.cloned.1.call-update) | async-done | bytes 1048592 | tf_op jit(solution)/shard_map/all_gather | solution.py:146
  142.8 2.3 copy.18
  145.1 31.1 %while.34 = (s32[]{:T(128)}, f32[2,640]{1,0:T(2,128)S(1)}, f32[2,640]{1,0:T(2,128)S(1)}, f32[2,640,64]{1,2,0:T(8,128)}, bf16[4096,128]{0,1:T(8,128)(2,1)}, /*ind...) while((s32[]{:T(128)}, f32[2,640]{1,0:T(2,128)S(1)}, ...), condition=%wide.region_3.0_spmd.clone, body=%wide.region_0.0_spmd.clone.sunk | while | flops 173267200 | bytes 12173539 | solution.py:36
  145.1 1.0 constant_dynamic-slice_fusion.6
  149.0 1.0 constant_dynamic-slice_fusion.6
  160.6 1.0 constant_dynamic-slice_fusion.6
  172.3 1.0 constant_dynamic-slice_fusion.6
  176.2 1.1 fusion.35
  177.3 1.6 broadcast_in_dim.29
  178.9 36.7 %while.35 = (s32[]{:T(128)}, f32[640,2,64]{0,2,1:T(8,128)S(1)}, bf16[4096,256]{0,1:T(8,128)(2,1)}, bf16[4096,128]{0,1:T(8,128)(2,1)}, bf16[640,2,64]{0,2,1:T(8,1...) while((s32[]{:T(128)}, f32[640,2,64]{0,2,1:T(8,128)S(1)}, ...), condition=%wide.region_6.0_spmd.clone, body=%wide.region_5.0_spmd.clone.sunk | while | flops 425492480 | bytes 14826685 | solution.py:36
  178.9 1.0 constant_dynamic-slice_fusion.7
  183.5 1.0 constant_dynamic-slice_fusion.7
  188.0 1.0 constant_dynamic-slice_fusion.7
  192.7 1.0 constant_dynamic-slice_fusion.7
  197.2 1.0 constant_dynamic-slice_fusion.7
  201.8 1.0 constant_dynamic-slice_fusion.7
  206.4 1.0 constant_dynamic-slice_fusion.7
  211.0 1.0 constant_dynamic-slice_fusion.7
  215.6 4.1 copy.21
  220.3 1.3 copy.25
  221.9 116.1 %reduce-scatter.10.cloned.1.call-done = bf16[128,256]{1,0:T(8,128)(2,1)} async-done(((bf16[4096,256]{1,0:T(8,128)(2,1)}), bf16[128,256]{1,0:T(8,128)(2,1)}) %reduce-scatter.10.cloned.1.call-update) | async-done | bytes 65552
  338.1 1.0 convolution_add_fusion.1
  339.1 1.0 fusion.28
  341.0 74.1 %reduce-scatter.14.cloned.1.call-done = bf16[128,512]{1,0:T(8,128)(2,1)} async-done(((bf16[1024,512]{1,0:T(8,128)(2,1)}), bf16[128,512]{1,0:T(8,128)(2,1)}) %reduce-scatter.14.cloned.1.call-update) | async-done | bytes 131088
  415.0 1.7 copy.26
  416.7 76.2 %reduce-scatter.12.cloned.1.call-done = bf16[128,128]{1,0:T(8,128)(2,1)} async-done(((bf16[1024,128]{1,0:T(8,128)(2,1)}), bf16[128,128]{1,0:T(8,128)(2,1)}) %reduce-scatter.12.cloned.1.call-update) | async-done | bytes 32784
  492.9 1.5 copy.24
  (168 shorter events, 57.6 us)
Async XLA Ops:
  7.2 4.1 copy-start
  7.2 6.0 %copy-start.7 = (bf16[128,1024]{1,0:T(8,128)(2,1)S(1)}, bf16[128,1024]{1,0:T(8,128)(2,1)}, u32[]{:S(2)}) copy-start(bf16[128,1024]{1,0:T(8,128)(2,1)} %param.17) | copy-start | bytes 786436
  7.2 6.0 %copy-start.8 = (bf16[128,1024]{1,0:T(8,128)(2,1)S(1)}, bf16[128,1024]{1,0:T(8,128)(2,1)}, u32[]{:S(2)}) copy-start(bf16[128,1024]{1,0:T(8,128)(2,1)} %param.18) | copy-start | bytes 786436
  7.2 6.0 %copy-start.6 = (bf16[512,1024]{1,0:T(8,128)(2,1)S(1)}, bf16[512,1024]{1,0:T(8,128)(2,1)}, u32[]{:S(2)}) copy-start(bf16[512,1024]{1,0:T(8,128)(2,1)} %param.19) | copy-start | bytes 3145732
  7.2 69.8 %all-gather.5.cloned.1.call-start = ((), (), s32[]{:S(2)}) async-start(), calls=%async_computation.4 | async-start | bytes 1081344 | tf_op jit(solution)/shard_map/all_gather | solution.py:147
  9.3 133.5 %all-gather.3.cloned.1.call-start = ((), (), s32[]{:S(2)}) async-start(), calls=%async_computation.3 | async-start | bytes 1081344 | tf_op jit(solution)/shard_map/all_gather | solution.py:146
  11.2 326.9 %reduce-scatter.10.cloned.1.call-start = ((), (), s32[]{:S(2)}) async-start(), calls=%async_computation.5 | async-start | bytes 2162688
  146.6 1.0 copy-start.2
  148.2 0.7 copy-start.3
  150.5 1.0 copy-start.2
  152.1 0.7 copy-start.3
  154.4 1.0 copy-start.2
  156.0 0.7 copy-start.3
  158.3 1.0 copy-start.2
  159.9 0.7 copy-start.3
  162.2 1.0 copy-start.2
  163.8 0.7 copy-start.3
  166.1 1.0 copy-start.2
  167.7 0.7 copy-start.3
  170.0 1.0 copy-start.2
  171.6 0.7 copy-start.3
  173.9 1.0 copy-start.2
  175.4 0.7 copy-start.3
  176.2 2.7 copy-start.1
  219.7 195.3 %reduce-scatter.14.cloned.1.call-start = ((), (), s32[]{:S(2)}) async-start(), calls=%async_computation.7 | async-start | bytes 1179648
  219.8 118.3 %copy-start.4 = (bf16[1024,128]{1,0:T(8,128)(2,1)S(1)}, bf16[1024,128]{1,0:T(8,128)(2,1)}, u32[]{:S(2)}) copy-start(bf16[1024,128]{1,0:T(8,128)(2,1)} %param.15) | copy-start | bytes 786436
  220.3 118.8 %copy-start.5 = (bf16[1024,128]{1,0:T(8,128)(2,1)S(1)}, bf16[1024,128]{1,0:T(8,128)(2,1)}, u32[]{:S(2)}) copy-start(bf16[1024,128]{1,0:T(8,128)(2,1)} %param.16) | copy-start | bytes 786436
  221.6 271.3 %reduce-scatter.12.cloned.1.call-start = ((), (), s32[]{:S(2)}) async-start(), calls=%async_computation.6 | async-start | bytes 294912
Sparse Core Ops, SparseCore 0:
  10.5 66.4 all-gather.4
  79.4 63.2 all-gather.2
  219.8 118.2 reduce-scatter.9
  342.4 72.6 reduce-scatter.13
  418.7 74.1 reduce-scatter.11
where the time goes:
time: 502 us; the launch traced here: 501 us
  waiting for transfers between devices  393 us (78%)
  local copies, waits for them, and re-layouts  41.2 us (8%)
  matrix products  40.4 us (8%)
  between operations  14 us (3%)
  other arithmetic  11.1 us (2%)
    unnamed x8, waiting for transfers between devices  266 us
    all_gather x1, waiting for transfers between devices, per_device(): lax.all_gather(key_local, 'tok', axis=0, tiled=True)  63.4 us
    all_gather x1, waiting for transfers between devices, per_device(): lax.all_gather(value_local, 'tok', axis=0, tiled=True)  63.3 us
    dynamic_slice x16, local copies, waits for them, and re-layouts, one_block(): value_part = lax.dynamic_slice_in_dim(value_rows, offset, width_now, 0)  15.8 us
    unnamed x21, local copies, waits for them, and re-layouts  14 us
  transfers between devices with their start and end apart: 5, of which 5 were waited for; matrix products, arithmetic and copies ran while one was open for 3% of the time, Pallas kernels for 0%

commit v1 on v0

v1 whole, which is shorter than its diff:
```python
import functools

import jax
import jax.numpy as jnp
from jax import lax
from jax.experimental import pallas as pl
from jax.experimental.pallas import tpu as pltpu
from jax.sharding import PartitionSpec as P

HEAD_DIM = 64
SCALE = HEAD_DIM ** (-0.5)
LOG2E = 1.4426950408889634
Y_LO, Z, CORES = 2, 8, 2
X, Y_HI = 4, 2
BF16 = jnp.bfloat16
F32 = jnp.float32


def tok_perm(move):
    pairs = []
    for yl in range(Y_LO):
        for z in range(Z):
            for core in range(CORES):
                yl2, z2, core2 = move(yl, z, core)
                pairs.append(
                    ((yl * Z + z) * CORES + core, (yl2 * Z + z2 % Z) * CORES + core2)
                )
    return pairs


def head_perm(move):
    pairs = []
    for x in range(X):
        for yh in range(Y_HI):
            x2, yh2 = move(x, yh)
            pairs.append((x * Y_HI + yh, (x2 % X) * Y_HI + yh2))
    return pairs


SWAP_Y = tok_perm(lambda yl, z, c: (1 - yl, z, c))
SWAP_CORE = tok_perm(lambda yl, z, c: (yl, z, 1 - c))
SPREAD_NEAR = tok_perm(lambda yl, z, c: (yl, z, 0) if c == 0 else (yl, z - 1, 1))
SPREAD_FAR = tok_perm(lambda yl, z, c: (yl, z - 1, 1) if c == 0 else (yl, z, 0))
RING_OUT = tok_perm(lambda yl, z, c: (yl, z + 1, 0) if c == 0 else (yl, z - 1, 1))
RING_BACK = tok_perm(lambda yl, z, c: (yl, z - 1, 0) if c == 0 else (yl, z + 1, 1))
RETURN_NEAR = tok_perm(lambda yl, z, c: (yl, z, 0) if c == 0 else (yl, z + 1, 1))
RETURN_FAR = tok_perm(lambda yl, z, c: (yl, z, 1) if c == 0 else (yl, z + 1, 0))
HOPS = 3
SHIFT_X = [head_perm(lambda x, yh, r=r: (x + r, yh)) for r in range(X)]
SWAP_YH = head_perm(lambda x, yh: (x, 1 - yh))


def dot(a, b, ca, cb):
    return lax.dot_general(a, b, (((ca,), (cb,)), ((), ())), preferred_element_type=F32)


def call(body, outs, args, name, flops=0, transcendentals=0, scratch=(), smem=0):
    nbytes = sum(a.size * a.dtype.itemsize for a in (*args, *outs))
    in_specs = [
        pl.BlockSpec(memory_space=pltpu.SMEM if i < smem else pltpu.VMEM)
        for i in range(len(args))
    ]
    return pl.pallas_call(
        body,
        out_shape=tuple(outs),
        in_specs=in_specs,
        out_specs=tuple(pl.BlockSpec(memory_space=pltpu.VMEM) for _ in outs),
        scratch_shapes=list(scratch),
        compiler_params=pltpu.CompilerParams(vmem_limit_bytes=28 << 20),
        cost_estimate=pl.CostEstimate(
            flops=flops, bytes_accessed=nbytes, transcendentals=transcendentals
        ),
        name=name,
    )(*args)


def sds(shape, dtype):
    return jax.ShapeDtypeStruct(shape, dtype)


def kv_kernel(rows, w_key, w_value, out):
    x = rows[...]
    out[:, 0:128] = dot(x, w_key[...], 1, 0).astype(BF16)
    out[:, 128:256] = dot(x, w_value[...], 1, 0).astype(BF16)


def qd_kernel(anchors, cells, grad_a, grad_c, w_query, w_out, out):
    na = anchors.shape[0]
    wq = w_query[...]
    wo = w_out[...]
    for lo, rows, grads in ((0, anchors, grad_a), (na, cells, grad_c)):
        hi = lo + rows.shape[0]
        out[lo:hi, 0:128] = dot(rows[...], wq, 1, 0).astype(BF16) * SCALE
        out[lo:hi, 128:256] = dot(grads[...], wo, 1, 1).astype(BF16)


def stats_block(kv, rhs, before, out):
    total = rhs.shape[0] // 2
    keys = kv[:, 0:128]
    values = kv[:, 128:256]
    for tile in range(0, total, 256):
        for h in range(2):
            lo = h * total + tile
            s = dot(keys, rhs[lo : lo + 256, 0:128], 1, 1)
            peak = jnp.max(s, axis=0, keepdims=True) * LOG2E
            if before is not None:
                old_peak = before[h : h + 1, tile : tile + 256]
                peak = jnp.maximum(peak, old_peak)
            e = jnp.exp2(s * LOG2E - peak)
            dp = dot(values, rhs[lo : lo + 256, 128:256], 1, 1)
            norm = jnp.sum(e, axis=0, keepdims=True)
            mass = jnp.sum(e * dp, axis=0, keepdims=True)
            if before is not None:
                factor = jnp.exp2(old_peak - peak)
                norm += factor * before[2 + h : 3 + h, tile : tile + 256]
                mass += factor * before[4 + h : 5 + h, tile : tile + 256]
            out[h : h + 1, tile : tile + 256] = peak
            out[2 + h : 3 + h, tile : tile + 256] = norm
            out[4 + h : 5 + h, tile : tile + 256] = mass
    out[6:8, :] = jnp.zeros((2, total), F32)


def first_stats_kernel(mine, theirs, kv, stats, rhs):
    half = mine.shape[0]
    lane = lax.broadcasted_iota(jnp.int32, (1, 256), 1)
    for h in range(2):
        keep = lane // HEAD_DIM % 2 == h
        for part, rows in enumerate((mine, theirs)):
            x = rows[...]
            lo = (2 * h + part) * half
            rhs[lo : lo + half, :] = jnp.where(keep, x, jnp.zeros_like(x))
    stats_block(kv, rhs, None, stats)


def next_stats_kernel(kv, rhs, before, stats):
    stats_block(kv, rhs, before, stats)


def merge_kernel(mine, theirs, out):
    half = mine.shape[1] // 2
    for a, b in ((0, half), (half, 0)):
        for h in range(2):
            m1 = mine[h : h + 1, a : a + half]
            m2 = theirs[h : h + 1, b : b + half]
            peak = jnp.maximum(m1, m2)
            f1 = jnp.exp2(m1 - peak)
            f2 = jnp.exp2(m2 - peak)
            norm = f1 * mine[2 + h : 3 + h, a : a + half] + f2 * theirs[2 + h : 3 + h, b : b + half]
            mass = f1 * mine[4 + h : 5 + h, a : a + half] + f2 * theirs[4 + h : 5 + h, b : b + half]
            out[h : h + 1, a : a + half] = peak + jnp.log(norm) * LOG2E
            out[2 + h : 3 + h, a : a + half] = mass / norm
    out[4:8, :] = jnp.zeros((4, 2 * half), F32)


def grads_kernel(has_before, is_last, *refs):
    kv, rhs, stats = refs[:3]
    refs = refs[3:]
    before = None
    if has_before:
        before, refs = refs[0], refs[1:]
    if is_last:
        dkv, dq_mine, dq_theirs, p_t, ds_t = refs
    else:
        dkv, dq, p_t, ds_t = refs
    total = rhs.shape[0] // 2
    half = total // 2
    n = kv.shape[0]
    keys_t = kv[:, 0:128].T
    step = 128
    for h in range(2):
        lo = h * total
        lse = stats[h : h + 1, :]
        delta = stats[2 + h : 3 + h, :]
        for c in range(0, n, step):
            s = dot(kv[c : c + step, 0:128], rhs[lo : lo + total, 0:128], 1, 1)
            p = jnp.exp2(s * LOG2E - lse)
            dp = dot(kv[c : c + step, 128:256], rhs[lo : lo + total, 128:256], 1, 1)
            ds = p * (dp - delta)
            p_t[c : c + step, lo : lo + total] = p.astype(BF16)
            ds_t[c : c + step, lo : lo + total] = ds.astype(BF16)
        out = slice(h * HEAD_DIM, (h + 1) * HEAD_DIM)
        part = dot(keys_t[out, :], ds_t[:, lo : lo + total], 1, 0)
        if has_before:
            part += before[out, :]
        if is_last:
            dq_mine[out, :] = part[:, :half]
            dq_theirs[out, :] = part[:, half:].astype(BF16)
        else:
            dq[out, :] = part
    dkv[:, 0:128] = dot(ds_t[...], rhs[:, 0:128], 1, 0).astype(BF16)
    dkv[:, 128:256] = dot(p_t[...], rhs[:, 128:256], 1, 0).astype(BF16)


def grads(kv, rhs, stats, before, is_last):
    total = rhs.shape[0] // 2
    n = kv.shape[0]
    args = [kv, rhs, stats] + ([] if before is None else [before])
    outs = [sds((n, 256), BF16)]
    if is_last:
        outs += [sds((128, total // 2), F32), sds((128, total // 2), BF16)]
    else:
        outs += [sds((128, total), F32)]
    return call(
        functools.partial(grads_kernel, before is not None, is_last),
        outs,
        args,
        "grads",
        flops=10 * n * 2 * total * 256,
        transcendentals=2 * n * total,
        scratch=[pltpu.VMEM((n, 2 * total), BF16), pltpu.VMEM((n, 2 * total), BF16)],
    )


def cells_kernel(place, mine, theirs, w_query, dq_anchors, *outs):
    na = mine.shape[1] - outs[0].shape[0]
    dq = ((mine[...] + theirs[...].astype(F32)) * SCALE).astype(BF16)
    dq_anchors[...] = dq[:, :na]
    width = outs[0].shape[1]
    for r, out in enumerate(outs):
        lo = pl.multiple_of(lax.rem(place[0] + r, X) * width, width)
        out[...] = dot(dq[:, na:], w_query[pl.ds(lo, width), :], 0, 1).astype(BF16)


def anchors_kernel(place, dq, dkv, more, w_query, w_key, w_value, *outs):
    width = outs[0].shape[1]
    total = (dkv[...] + more[...].astype(F32)).astype(BF16)
    for r, out in enumerate(outs):
        lo = pl.multiple_of(lax.rem(place[0] + r, X) * width, width)
        acc = dot(dq[...], w_query[pl.ds(lo, width), :], 0, 1)
        acc += dot(total[:, 0:128], w_key[pl.ds(lo, width), :], 1, 1)
        acc += dot(total[:, 128:256], w_value[pl.ds(lo, width), :], 1, 1)
        out[...] = acc.astype(BF16)


def split_kernel(place, a, b, c, d, mine, theirs):
    def terms(lo):
        cols = slice(lo, lo + 128)
        return (a[:, cols].astype(F32) + b[:, cols].astype(F32)) + (
            c[:, cols].astype(F32) + d[:, cols].astype(F32)
        )

    low, high = terms(0), terms(128)
    first = place[1] == 0
    mine[...] = jnp.where(first, low, high)
    theirs[...] = jnp.where(first, high, low).astype(BF16)


def over_heads(place, chunks):
    rows = chunks[0].shape[0]
    got = [lax.ppermute(chunks[r], "head", SHIFT_X[r]) for r in range(1, X)]
    mine, theirs = call(
        split_kernel,
        [sds((rows, 128), F32), sds((rows, 128), BF16)],
        [place, chunks[0], *got],
        "split",
        smem=1,
    )
    more = lax.ppermute(theirs, "head", SWAP_YH)
    return (mine + more.astype(F32)).astype(BF16)


def per_device(anchors, cells, w_query, w_key, w_value, w_out, grad_a, grad_c):
    na, nc, d = anchors.shape[0], cells.shape[0], anchors.shape[1]
    rows = na + nc
    total = 2 * rows
    head = lax.axis_index("head")
    place = jnp.stack([head // Y_HI, head % Y_HI]).astype(jnp.int32)

    (kv,) = call(
        kv_kernel,
        [sds((na, 256), BF16)],
        [anchors, w_key, w_value],
        "kv",
        flops=2 * na * d * 256,
    )
    kv_pair = jnp.concatenate([kv, lax.ppermute(kv, "tok", SWAP_Y)], axis=0)
    block = jnp.concatenate(
        [
            lax.ppermute(kv_pair, "tok", SPREAD_NEAR),
            lax.ppermute(kv_pair, "tok", SPREAD_FAR),
        ],
        axis=0,
    )
    blocks = [block]
    for _ in range(HOPS):
        blocks.append(lax.ppermute(blocks[-1], "tok", RING_OUT))

    (mine,) = call(
        qd_kernel,
        [sds((rows, 256), BF16)],
        [anchors, cells, grad_a, grad_c, w_query, w_out],
        "qd",
        flops=2 * rows * d * 256,
    )
    theirs = lax.ppermute(mine, "tok", SWAP_CORE)

    n = block.shape[0]
    cost = dict(flops=4 * n * 2 * total * 256, transcendentals=2 * n * total)
    stats, rhs = call(
        first_stats_kernel,
        [sds((8, total), F32), sds((2 * total, 256), BF16)],
        [mine, theirs, blocks[0]],
        "stats0",
        **cost,
    )
    for kv_block in blocks[1:]:
        (stats,) = call(
            next_stats_kernel, [sds((8, total), F32)], [kv_block, rhs, stats], "stats", **cost
        )
    (stats,) = call(
        merge_kernel,
        [sds((8, total), F32)],
        [stats, lax.ppermute(stats, "tok", SWAP_CORE)],
        "merge",
    )

    dq = None
    arrived = None
    for k in range(HOPS, -1, -1):
        dkv, *dq = grads(blocks[k], rhs, stats, dq, k == 0)
        if arrived is not None:
            dkv = (dkv.astype(F32) + arrived.astype(F32)).astype(BF16)
        if k > 0:
            arrived = lax.ppermute(dkv, "tok", RING_BACK)
            dq = dq[0]

    dq_mine, dq_theirs = dq
    dq_theirs = lax.ppermute(dq_theirs, "tok", SWAP_CORE)
    width = d // X
    dq_anchors, *chunks = call(
        cells_kernel,
        [sds((128, na), BF16)] + [sds((nc, width), BF16)] * X,
        [place, dq_mine, dq_theirs, w_query],
        "cells",
        flops=2 * nc * 128 * d,
        smem=1,
    )
    cell_grad = over_heads(place, chunks)

    near = lax.ppermute(dkv[: n // 2], "tok", RETURN_NEAR)
    far = lax.ppermute(dkv[n // 2 :], "tok", RETURN_FAR)
    pair = near.astype(F32) + far.astype(F32)
    more = lax.ppermute(pair[na:].astype(BF16), "tok", SWAP_Y)
    chunks = call(
        anchors_kernel,
        [sds((na, width), BF16)] * X,
        [place, dq_anchors, pair[:na], more, w_query, w_key, w_value],
        "anchors",
        flops=2 * na * 128 * d * 3,
        smem=1,
    )
    anchor_grad = over_heads(place, chunks)
    return (anchor_grad, cell_grad)


def solution(mesh):
    return jax.shard_map(
        per_device,
        mesh=mesh,
        in_specs=(
            P("tok", None),
            P("tok", None),
            P(None, "head"),
            P(None, "head"),
            P(None, "head"),
            P("head", None),
            P("tok", None),
            P("tok", None),
        ),
        out_specs=(P("tok", "head"), P("tok", "head")),
        check_vma=False,
    )
```

time: 502 us -> 109 us (0.22)
  waiting for transfers between devices: 393 us -> 37.9 us
  matrix products: 40.4 us -> 0 us
  starting transfers between devices: 0.2 us -> 36.5 us
  local copies, waits for them, and re-layouts: 41.2 us -> 5.13 us
  Pallas kernels: 0 us -> 26.9 us
  between operations: 14 us -> 0.86 us
  other arithmetic: 11.1 us -> 1.65 us
    unnamed x8 -> x0, waiting for transfers between devices: 266 us -> none
    all_gather x2 -> x0, waiting for transfers between devices: 127 us -> none  [the longest x1 63.4 us: per_device(): lax.all_gather(key_local, 'tok', axis=0, tiled=True)]
    dot_general x64 -> x0, matrix products: 40.4 us -> none  [the longest x8 6.07 us: score_terms(): jnp.einsum('rhc,khc->hrk', grad_heads, value_heads, preferred_element_typ...]
    ppermute x0 -> x23, waiting for transfers between devices: none -> 37.9 us  [the longest x6 14 us: over_heads(): got = [lax.ppermute(chunks[r], 'head', SHIFT_X[r]) for r in range(1, X)]]
    ppermute x0 -> x23, starting transfers between devices: none -> 36.5 us  [the longest x3 10.4 us: per_device(): arrived = lax.ppermute(dkv, 'tok', RING_BACK)]
    pallas_call x0 -> x15, Pallas kernels: none -> 26.9 us  [call(): pl.pallas_call(body, out_shape=tuple(outs), in_specs=in_specs, out_specs=...]
    dynamic_slice x16 -> x0, local copies, waits for them, and re-layouts: 15.8 us -> none  [one_block(): value_part = lax.dynamic_slice_in_dim(value_rows, offset, width_now, 0)]
    while x40 -> x0, local copies, waits for them, and re-layouts: 9.71 us -> none
  transfers between devices with their start and end apart: 5 -> 23, of which waited for: 5 -> 17; matrix products, arithmetic and copies ran while one was open for 3% -> 1% of each run, Pallas kernels for 0% -> 19%
where the time goes in v1:
time: 109 us
  waiting for transfers between devices  37.9 us (35%)
  starting transfers between devices  36.5 us (33%)
  Pallas kernels  26.9 us (25%)
  local copies, waits for them, and re-layouts  5.13 us (5%)
  other arithmetic  1.65 us (2%)
    pallas_call x15, Pallas kernels, call(): pl.pallas_call(body, out_shape=tuple(outs), in_specs=in_specs, out_specs=...  26.9 us
    ppermute x6, waiting for transfers between devices, over_heads(): got = [lax.ppermute(chunks[r], 'head', SHIFT_X[r]) for r in range(1, X)]  14 us
    ppermute x3, starting transfers between devices, per_device(): arrived = lax.ppermute(dkv, 'tok', RING_BACK)  10.4 us
    ppermute x3, waiting for transfers between devices, per_device(): blocks.append(lax.ppermute(blocks[-1], 'tok', RING_OUT))  9.53 us
    ppermute x6, starting transfers between devices, over_heads(): got = [lax.ppermute(chunks[r], 'head', SHIFT_X[r]) for r in range(1, X)]  6.47 us
    ppermute x1, starting transfers between devices, per_device(): lax.ppermute(kv_pair, 'tok', SPREAD_FAR)  6.13 us
    unnamed x21, local copies, waits for them, and re-layouts  5.08 us
    ppermute x2, waiting for transfers between devices, over_heads(): more = lax.ppermute(theirs, 'head', SWAP_YH)  4.38 us
  transfers between devices with their start and end apart: 23, of which 17 were waited for; matrix products, arithmetic and copies ran while one was open for 1% of the time, Pallas kernels for 19%

profile of v1, /device:TPU:6, one launch (start us, length us, event | category | flops | bytes accessed | tf_op | source)
XLA Modules:
  0.0 108.9 jit_solution(6403519075417915382)
XLA Ops:
  3.8 1.7 %collective-permute-start = (bf16[128,256]{1,0:T(8,128)(2,1)S(1)}, bf16[128,256]{1,0:T(8,128)(2,1)S(1)}, u32[]{:S(2)}, u32[]{:S(2)}) collective-permute-start(bf16[128,256]{1,0:T(8,128)(2,1)S(1)} %kv.1), channel_id=1, source_target_pairs={{0,16},{1,17},{2,18},{3,19},{4,20},{5,21},{6,22},{7,23},{8,24},{9,... | collective-permute-start | bytes 196616 | tf_op jit(solution)/shard_map/ppermute | solution.py:276
  5.5 2.7 %collective-permute-done = bf16[128,256]{1,0:T(8,128)(2,1)S(1)} collective-permute-done((bf16[128,256]{1,0:T(8,128)(2,1)S(1)}, bf16[128,256]{1,0:T(8,128)(2,1)S(1)}, u32[]{:S(2)}, u32[]{:S(2)}) %collective-permute-start) | collective-permute-done | bytes 65568 | tf_op jit(solution)/shard_map/ppermute | solution.py:276
  8.9 6.1 %collective-permute-start.2 = (bf16[256,256]{1,0:T(8,128)(2,1)S(1)}, bf16[256,256]{1,0:T(8,128)(2,1)S(1)}, u32[]{:S(2)}, u32[]{:S(2)}) collective-permute-start(bf16[256,256]{1,0:T(8,128)(2,1)S(1)} %pad_maximum_fusion), channel_id=1, source_target_pairs={{0,15},{1,0},{2,1},{3,2},{4,3},{5,4},{6,5},{7,6},{8,7},{9,8},{10,9... | collective-permute-start | bytes 393224 | tf_op jit(solution)/shard_map/ppermute | solution.py:280
  15.0 2.5 %collective-permute-done.2 = bf16[256,256]{1,0:T(8,128)(2,1)S(1)} collective-permute-done((bf16[256,256]{1,0:T(8,128)(2,1)S(1)}, bf16[256,256]{1,0:T(8,128)(2,1)S(1)}, u32[]{:S(2)}, u32[]{:S(2)}) %collective-permute-start.2) | collective-permute-done | bytes 131104 | tf_op jit(solution)/shard_map/ppermute | solution.py:280
  18.6 1.2 %copy-done.6 = bf16[512,1024]{1,0:T(8,128)(2,1)S(1)} copy-done((bf16[512,1024]{1,0:T(8,128)(2,1)S(1)}, bf16[512,1024]{1,0:T(8,128)(2,1)}, u32[]{:S(2)}) %copy-start.6) | copy-done | bytes 1048600
  21.6 2.3 %collective-permute-start.3 = (bf16[640,256]{1,0:T(8,128)(2,1)S(1)}, bf16[640,256]{1,0:T(8,128)(2,1)S(1)}, u32[]{:S(2)}, u32[]{:S(2)}) collective-permute-start(bf16[640,256]{1,0:T(8,128)(2,1)S(1)} %qd.1.mine), channel_id=1, source_target_pairs={{0,1},{1,0},{2,3},{3,2},{4,5},{5,4},{6,7},{7,6},{8,9},{9,8},{10,11... | collective-permute-start | bytes 983048 | tf_op jit(solution)/shard_map/ppermute | solution.py:295
  24.0 1.2 %collective-permute-done.4.kv.refs_0_ = bf16[512,256]{1,0:T(8,128)(2,1)S(1)} collective-permute-done((bf16[512,256]{1,0:T(8,128)(2,1)S(1)}, bf16[512,256]{1,0:T(8,128)(2,1)S(1)}, u32[]{:S(2)}, u32[]{:S(2)}) %collective-permute-start.4) | collective-permute-done | bytes 262176 | tf_op jit(solution)/shard_map/ppermute | solution.py:286
  25.2 7.6 %collective-permute-done.5.kv.refs_0_ = bf16[512,256]{1,0:T(8,128)(2,1)S(1)} collective-permute-done((bf16[512,256]{1,0:T(8,128)(2,1)S(1)}, bf16[512,256]{1,0:T(8,128)(2,1)S(1)}, u32[]{:S(2)}, u32[]{:S(2)}) %collective-permute-start.5) | collective-permute-done | bytes 262176 | tf_op jit(solution)/shard_map/ppermute | solution.py:286
  32.8 2.4 %stats0.1 = (f32[8,1280]{1,0:T(8,128)S(1)}, bf16[2560,256]{1,0:T(8,128)(2,1)S(1)}) custom-call(bf16[640,256]{1,0:T(8,128)(2,1)S(1)} %qd.1.mine, bf16[640,256]{1,0:T(8,128)(2,1)S(1)} %collective-permute-done.3.theirs, bf16[512,256]{1,0:T(8,128)(2,1)S(1)} %constant_dynamic-update-slice_fusion.kv.refs_0_), custom_call_target="tpu_custom_call" | custom-call | flops 1342177280 | bytes 2269184 | tf_op jit(solution)/shard_map/stats0/pallas_call | solution.py:63
  35.3 2.2 %stats.3.before = f32[8,1280]{1,0:T(8,128)S(1)} custom-call(bf16[512,256]{1,0:T(8,128)(2,1)S(1)} %collective-permute-done.4.kv.refs_0_, bf16[2560,256]{1,0:T(8,128)(2,1)S(1)} %get-tuple-element.26.rhs.refs_1_, f32[8,1280]{1,0:T(8,128)S(1)} %get-tuple-element.27.before), custom_call_target="tpu_custom_call" | custom-call | flops 1342177280 | bytes 1654784 | tf_op jit(solution)/shard_map/stats/pallas_call | solution.py:63
  37.5 2.2 %stats.4.before = f32[8,1280]{1,0:T(8,128)S(1)} custom-call(bf16[512,256]{1,0:T(8,128)(2,1)S(1)} %collective-permute-done.5.kv.refs_0_, bf16[2560,256]{1,0:T(8,128)(2,1)S(1)} %get-tuple-element.26.rhs.refs_1_, f32[8,1280]{1,0:T(8,128)S(1)} %stats.3.before), custom_call_target="tpu_custom_call" | custom-call | flops 1342177280 | bytes 1654784 | tf_op jit(solution)/shard_map/stats/pallas_call | solution.py:63
  40.4 2.2 %stats.5.mine = f32[8,1280]{1,0:T(8,128)S(1)} custom-call(bf16[512,256]{1,0:T(8,128)(2,1)S(1)} %collective-permute-done.6.kv.refs_0_, bf16[2560,256]{1,0:T(8,128)(2,1)S(1)} %get-tuple-element.26.rhs.refs_1_, f32[8,1280]{1,0:T(8,128)S(1)} %stats.4.before), custom_call_target="tpu_custom_call" | custom-call | flops 1342177280 | bytes 1654784 | tf_op jit(solution)/shard_map/stats/pallas_call | solution.py:63
  44.0 3.4 %grads.4 = (bf16[512,256]{1,0:T(8,128)(2,1)S(1)}, f32[128,1280]{1,0:T(8,128)S(1)}) custom-call(bf16[512,256]{1,0:T(8,128)(2,1)S(1)} %collective-permute-done.6.kv.refs_0_, bf16[2560,256]{1,0:T(8,128)(2,1)S(1)} %get-tuple-element.26.rhs.refs_1_, f32[8,1280]{1,0:T(8,128)S(1)} %merge.1.refs_2_), custom_call_target="tpu_custom_call" | custom-call | flops 3355443200 | bytes 2531328 | tf_op jit(solution)/shard_map/grads/pallas_call | solution.py:63
  47.3 2.8 %collective-permute-start.9 = (bf16[512,256]{1,0:T(8,128)(2,1)S(1)}, bf16[512,256]{1,0:T(8,128)(2,1)S(1)}, u32[]{:S(2)}, u32[]{:S(2)}) collective-permute-start(bf16[512,256]{1,0:T(8,128)(2,1)S(1)} %get-tuple-element.37), channel_id=1, source_target_pairs={{0,14},{1,3},{2,0},{3,5},{4,2},{5,7},{6,4},{7,9},{8,6},{9,11},{10,... | collective-permute-start | bytes 786440 | tf_op jit(solution)/shard_map/ppermute | solution.py:324
  50.2 3.4 %grads.5 = (bf16[512,256]{1,0:T(8,128)(2,1)S(1)}, f32[128,1280]{1,0:T(8,128)S(1)}) custom-call(bf16[512,256]{1,0:T(8,128)(2,1)S(1)} %collective-permute-done.5.kv.refs_0_, bf16[2560,256]{1,0:T(8,128)(2,1)S(1)} %get-tuple-element.26.rhs.refs_1_, f32[8,1280]{1,0:T(8,128)S(1)} %merge.1.refs_2_, f32[128,1280]{1,0:T(8,128)S(1)} %get-tuple-element.28.refs_3_), custom_call_target="tpu_custom_call" | custom-call | flops 3355443200 | bytes 3186688 | tf_op jit(solution)/shard_map/grads/pallas_call | solution.py:63
  54.1 3.8 %collective-permute-start.10 = (bf16[512,256]{1,0:T(8,128)(2,1)S(1)}, bf16[512,256]{1,0:T(8,128)(2,1)S(1)}, u32[]{:S(2)}, u32[]{:S(2)}) collective-permute-start(bf16[512,256]{1,0:T(8,128)(2,1)S(1)} %add_convert_fusion.2), channel_id=1, source_target_pairs={{0,14},{1,3},{2,0},{3,5},{4,2},{5,7},{6,4},{7,9},{8,6},{9,11},{10,... | collective-permute-start | bytes 786440 | tf_op jit(solution)/shard_map/ppermute | solution.py:324
  57.9 3.4 %grads.6 = (bf16[512,256]{1,0:T(8,128)(2,1)S(1)}, f32[128,1280]{1,0:T(8,128)S(1)}) custom-call(bf16[512,256]{1,0:T(8,128)(2,1)S(1)} %collective-permute-done.4.kv.refs_0_, bf16[2560,256]{1,0:T(8,128)(2,1)S(1)} %get-tuple-element.26.rhs.refs_1_, f32[8,1280]{1,0:T(8,128)S(1)} %merge.1.refs_2_, f32[128,1280]{1,0:T(8,128)S(1)} %get-tuple-element.29.refs_3_), custom_call_target="tpu_custom_call" | custom-call | flops 3355443200 | bytes 3186688 | tf_op jit(solution)/shard_map/grads/pallas_call | solution.py:63
  61.9 3.8 %collective-permute-start.11 = (bf16[512,256]{1,0:T(8,128)(2,1)S(1)}, bf16[512,256]{1,0:T(8,128)(2,1)S(1)}, u32[]{:S(2)}, u32[]{:S(2)}) collective-permute-start(bf16[512,256]{1,0:T(8,128)(2,1)S(1)} %add_convert_fusion.1), channel_id=1, source_target_pairs={{0,14},{1,3},{2,0},{3,5},{4,2},{5,7},{6,4},{7,9},{8,6},{9,11},{10,... | collective-permute-start | bytes 786440 | tf_op jit(solution)/shard_map/ppermute | solution.py:324
  65.6 3.4 %grads.7 = (bf16[512,256]{1,0:T(8,128)(2,1)S(1)}, f32[128,640]{1,0:T(8,128)S(1)}, bf16[128,640]{1,0:T(8,128)(2,1)S(1)}) custom-call(bf16[512,256]{1,0:T(8,128)(2,1)S(1)} %constant_dynamic-update-slice_fusion.kv.refs_0_, bf16[2560,256]{1,0:T(8,128)(2,1)S(1)} %get-tuple-element.26.rhs.refs_1_, f32[8,1280]{1,0:T(8,128)S(1)} %merge.1.refs_2_, ...), custom_call_target="tpu_custom_call" | custom-call | flops 3355443200 | bytes 3022848 | tf_op jit(solution)/shard_map/grads/pallas_call | solution.py:63
  70.3 1.3 %collective-permute-start.13 = (bf16[256,256]{1,0:T(8,128)(2,1)S(1)}, bf16[256,256]{1,0:T(8,128)(2,1)S(1)}, u32[]{:S(2)}, u32[]{:S(2)}) collective-permute-start(bf16[256,256]{1,0:T(8,128)(2,1)S(1)} %get-tuple-element.51), channel_id=1, source_target_pairs={{0,1},{1,2},{2,3},{3,4},{4,5},{5,6},{6,7},{7,8},{8,9},{9,10},{10,1... | collective-permute-start | bytes 393224 | tf_op jit(solution)/shard_map/ppermute | solution.py:341
  73.6 2.4 %collective-permute-start.20 = (bf16[512,256]{1,0:T(8,128)(2,1)S(1)}, bf16[512,256]{1,0:T(8,128)(2,1)S(1)}, u32[]{:S(2)}, u32[]{:S(2)}) collective-permute-start(bf16[512,256]{1,0:T(8,128)(2,1)S(1)} %get-tuple-element.46), channel_id=1, source_target_pairs={{0,128},{32,160},{64,192},{96,224},{128,0},{160,32},{192,64},{224,... | collective-permute-start | bytes 786440 | tf_op jit(solution)/shard_map/ppermute | solution.py:250
  76.0 2.2 %collective-permute-done.13 = bf16[256,256]{1,0:T(8,128)(2,1)S(1)} collective-permute-done((bf16[256,256]{1,0:T(8,128)(2,1)S(1)}, bf16[256,256]{1,0:T(8,128)(2,1)S(1)}, u32[]{:S(2)}, u32[]{:S(2)}) %collective-permute-start.13) | collective-permute-done | bytes 131104 | tf_op jit(solution)/shard_map/ppermute | solution.py:341
  78.3 1.7 %collective-permute-start.14 = (bf16[128,256]{1,0:T(8,128)(2,1)S(1)}, bf16[128,256]{1,0:T(8,128)(2,1)S(1)}, u32[]{:S(2)}, u32[]{:S(2)}) collective-permute-start(bf16[128,256]{1,0:T(8,128)(2,1)S(1)} %slice.22), channel_id=1, source_target_pairs={{0,16},{1,17},{2,18},{3,19},{4,20},{5,21},{6,22},{7,23},{8,24},{9,... | collective-permute-start | bytes 196616 | tf_op jit(solution)/shard_map/ppermute | solution.py:343
  79.9 2.3 %collective-permute-done.19.b = bf16[512,256]{1,0:T(8,128)(2,1)S(1)} collective-permute-done((bf16[512,256]{1,0:T(8,128)(2,1)S(1)}, bf16[512,256]{1,0:T(8,128)(2,1)S(1)}, u32[]{:S(2)}, u32[]{:S(2)}) %collective-permute-start.19) | collective-permute-done | bytes 262176 | tf_op jit(solution)/shard_map/ppermute | solution.py:250
  82.3 2.1 %collective-permute-done.20.c = bf16[512,256]{1,0:T(8,128)(2,1)S(1)} collective-permute-done((bf16[512,256]{1,0:T(8,128)(2,1)S(1)}, bf16[512,256]{1,0:T(8,128)(2,1)S(1)}, u32[]{:S(2)}, u32[]{:S(2)}) %collective-permute-start.20) | collective-permute-done | bytes 262176 | tf_op jit(solution)/shard_map/ppermute | solution.py:250
  84.3 4.3 %collective-permute-done.21.d = bf16[512,256]{1,0:T(8,128)(2,1)S(1)} collective-permute-done((bf16[512,256]{1,0:T(8,128)(2,1)S(1)}, bf16[512,256]{1,0:T(8,128)(2,1)S(1)}, u32[]{:S(2)}, u32[]{:S(2)}) %collective-permute-start.21) | collective-permute-done | bytes 262176 | tf_op jit(solution)/shard_map/ppermute | solution.py:250
  89.3 3.3 %collective-permute-start.22 = (bf16[512,128]{1,0:T(8,128)(2,1)S(1)}, bf16[512,128]{1,0:T(8,128)(2,1)S(1)}, u32[]{:S(2)}, u32[]{:S(2)}) collective-permute-start(bf16[512,128]{1,0:T(8,128)(2,1)S(1)} %get-tuple-element.49), channel_id=1, source_target_pairs={{0,32},{32,0},{64,96},{96,64},{128,160},{160,128},{192,224},{224,1... | collective-permute-start | bytes 393224 | tf_op jit(solution)/shard_map/ppermute | solution.py:258
  94.6 2.1 %collective-permute-start.16 = (bf16[128,256]{1,0:T(8,128)(2,1)S(1)}, bf16[128,256]{1,0:T(8,128)(2,1)S(1)}, u32[]{:S(2)}, u32[]{:S(2)}) collective-permute-start(bf16[128,256]{1,0:T(8,128)(2,1)S(1)} %get-tuple-element.40), channel_id=1, source_target_pairs={{0,128},{32,160},{64,192},{96,224},{128,0},{160,32},{192,64},{224,... | collective-permute-start | bytes 196616 | tf_op jit(solution)/shard_map/ppermute | solution.py:250
  96.8 1.3 %collective-permute-done.15.b = bf16[128,256]{1,0:T(8,128)(2,1)S(1)} collective-permute-done((bf16[128,256]{1,0:T(8,128)(2,1)S(1)}, bf16[128,256]{1,0:T(8,128)(2,1)S(1)}, u32[]{:S(2)}, u32[]{:S(2)}) %collective-permute-start.15) | collective-permute-done | bytes 65568 | tf_op jit(solution)/shard_map/ppermute | solution.py:250
  98.1 2.9 %collective-permute-done.16.c = bf16[128,256]{1,0:T(8,128)(2,1)S(1)} collective-permute-done((bf16[128,256]{1,0:T(8,128)(2,1)S(1)}, bf16[128,256]{1,0:T(8,128)(2,1)S(1)}, u32[]{:S(2)}, u32[]{:S(2)}) %collective-permute-start.16) | collective-permute-done | bytes 65568 | tf_op jit(solution)/shard_map/ppermute | solution.py:250
  101.0 1.2 %collective-permute-done.17.d = bf16[128,256]{1,0:T(8,128)(2,1)S(1)} collective-permute-done((bf16[128,256]{1,0:T(8,128)(2,1)S(1)}, bf16[128,256]{1,0:T(8,128)(2,1)S(1)}, u32[]{:S(2)}, u32[]{:S(2)}) %collective-permute-start.17) | collective-permute-done | bytes 65568 | tf_op jit(solution)/shard_map/ppermute | solution.py:250
  103.9 4.4 %collective-permute-done.18 = bf16[128,128]{1,0:T(8,128)(2,1)S(1)} collective-permute-done((bf16[128,128]{1,0:T(8,128)(2,1)S(1)}, bf16[128,128]{1,0:T(8,128)(2,1)S(1)}, u32[]{:S(2)}, u32[]{:S(2)}) %collective-permute-start.18) | collective-permute-done | bytes 32800 | tf_op jit(solution)/shard_map/ppermute | solution.py:258
  (62 shorter events, 18.4 us)
Async XLA Ops:
  0.6 18.0 %copy-start = (bf16[1024,128]{1,0:T(8,128)(2,1)S(1)}, bf16[1024,128]{1,0:T(8,128)(2,1)}, u32[]{:S(2)}) copy-start(bf16[1024,128]{1,0:T(8,128)(2,1)} %w_query.5) | copy-start | bytes 786436
  0.6 1.0 copy-start.1
  1.6 0.9 copy-start.3
  2.6 0.9 copy-start.7
  3.5 15.1 %copy-start.5 = (bf16[512,1024]{1,0:T(8,128)(2,1)S(1)}, bf16[512,1024]{1,0:T(8,128)(2,1)}, u32[]{:S(2)}) copy-start(bf16[512,1024]{1,0:T(8,128)(2,1)} %cells.2) | copy-start | bytes 3145732
  3.5 15.1 %copy-start.8 = (bf16[128,1024]{1,0:T(8,128)(2,1)S(1)}, bf16[128,1024]{1,0:T(8,128)(2,1)}, u32[]{:S(2)}) copy-start(bf16[128,1024]{1,0:T(8,128)(2,1)} %grad_a.1) | copy-start | bytes 786436
  3.8 4.4 %collective-permute-start = (bf16[128,256]{1,0:T(8,128)(2,1)S(1)}, bf16[128,256]{1,0:T(8,128)(2,1)S(1)}, u32[]{:S(2)}, u32[]{:S(2)}) collective-permute-start(bf16[128,256]{1,0:T(8,128)(2,1)S(1)} %kv.1), channel_id=1, source_target_pairs={{0,16},{1,17},{2,18},{3,19},{4,20},{5,21},{6,22},{7,23},{8,24},{9,... | collective-permute-start | bytes 196616 | tf_op jit(solution)/shard_map/ppermute | solution.py:276
  8.2 6.8 %collective-permute-start.1 = (bf16[256,256]{1,0:T(8,128)(2,1)S(1)}, bf16[256,256]{1,0:T(8,128)(2,1)S(1)}, u32[]{:S(2)}, u32[]{:S(2)}) collective-permute-start(bf16[256,256]{1,0:T(8,128)(2,1)S(1)} %pad_maximum_fusion), channel_id=1, source_target_pairs={{0,0},{1,15},{2,2},{3,1},{4,4},{5,3},{6,6},{7,5},{8,8},{9,7},{10,1... | collective-permute-start | bytes 393224 | tf_op jit(solution)/shard_map/ppermute | solution.py:279
  8.9 8.7 %collective-permute-start.2 = (bf16[256,256]{1,0:T(8,128)(2,1)S(1)}, bf16[256,256]{1,0:T(8,128)(2,1)S(1)}, u32[]{:S(2)}, u32[]{:S(2)}) collective-permute-start(bf16[256,256]{1,0:T(8,128)(2,1)S(1)} %pad_maximum_fusion), channel_id=1, source_target_pairs={{0,15},{1,0},{2,1},{3,2},{4,3},{5,4},{6,5},{7,6},{8,7},{9,8},{10,9... | collective-permute-start | bytes 393224 | tf_op jit(solution)/shard_map/ppermute | solution.py:280
  17.6 7.7 %collective-permute-start.4 = (bf16[512,256]{1,0:T(8,128)(2,1)S(1)}, bf16[512,256]{1,0:T(8,128)(2,1)S(1)}, u32[]{:S(2)}, u32[]{:S(2)}) collective-permute-start(bf16[512,256]{1,0:T(8,128)(2,1)S(1)} %constant_dynamic-update-slice_fusion.kv.refs_0_), channel_id=1, source_target_pairs={{0,2},{1,15},{2,4},{3,1},{4,6},{5,3},{6,8},{7,5},{8,10},{9,7},{10,... | collective-permute-start | bytes 786440 | tf_op jit(solution)/shard_map/ppermute | solution.py:286
  18.6 1.2 %copy-start.6 = (bf16[512,1024]{1,0:T(8,128)(2,1)S(1)}, bf16[512,1024]{1,0:T(8,128)(2,1)}, u32[]{:S(2)}) copy-start(bf16[512,1024]{1,0:T(8,128)(2,1)} %grad_c.1) | copy-start | bytes 3145732
  21.6 11.2 %collective-permute-start.3 = (bf16[640,256]{1,0:T(8,128)(2,1)S(1)}, bf16[640,256]{1,0:T(8,128)(2,1)S(1)}, u32[]{:S(2)}, u32[]{:S(2)}) collective-permute-start(bf16[640,256]{1,0:T(8,128)(2,1)S(1)} %qd.1.mine), channel_id=1, source_target_pairs={{0,1},{1,0},{2,3},{3,2},{4,5},{5,4},{6,7},{7,6},{8,9},{9,8},{10,11... | collective-permute-start | bytes 983048 | tf_op jit(solution)/shard_map/ppermute | solution.py:295
  25.2 7.6 %collective-permute-start.5 = (bf16[512,256]{1,0:T(8,128)(2,1)S(1)}, bf16[512,256]{1,0:T(8,128)(2,1)S(1)}, u32[]{:S(2)}, u32[]{:S(2)}) collective-permute-start(bf16[512,256]{1,0:T(8,128)(2,1)S(1)} %collective-permute-done.4.kv.refs_0_), channel_id=1, source_target_pairs={{0,2},{1,15},{2,4},{3,1},{4,6},{5,3},{6,8},{7,5},{8,10},{9,7},{10,... | collective-permute-start | bytes 786440 | tf_op jit(solution)/shard_map/ppermute | solution.py:286
  32.8 7.6 %collective-permute-start.6 = (bf16[512,256]{1,0:T(8,128)(2,1)S(1)}, bf16[512,256]{1,0:T(8,128)(2,1)S(1)}, u32[]{:S(2)}, u32[]{:S(2)}) collective-permute-start(bf16[512,256]{1,0:T(8,128)(2,1)S(1)} %collective-permute-done.5.kv.refs_0_), channel_id=1, source_target_pairs={{0,2},{1,15},{2,4},{3,1},{4,6},{5,3},{6,8},{7,5},{8,10},{9,7},{10,... | collective-permute-start | bytes 786440 | tf_op jit(solution)/shard_map/ppermute | solution.py:286
  42.6 1.3 %collective-permute-start.7 = (f32[8,1280]{1,0:T(8,128)S(1)}, f32[8,1280]{1,0:T(8,128)S(1)}, u32[]{:S(2)}, u32[]{:S(2)}) collective-permute-start(f32[8,1280]{1,0:T(8,128)S(1)} %stats.5.mine), channel_id=1, source_target_pairs={{0,1},{1,0},{2,3},{3,2},{4,5},{5,4},{6,7},{7,6},{8,9},{9,8},{10,11... | collective-permute-start | bytes 122888 | tf_op jit(solution)/shard_map/ppermute | solution.py:313
  47.3 6.7 %collective-permute-start.9 = (bf16[512,256]{1,0:T(8,128)(2,1)S(1)}, bf16[512,256]{1,0:T(8,128)(2,1)S(1)}, u32[]{:S(2)}, u32[]{:S(2)}) collective-permute-start(bf16[512,256]{1,0:T(8,128)(2,1)S(1)} %get-tuple-element.37), channel_id=1, source_target_pairs={{0,14},{1,3},{2,0},{3,5},{4,2},{5,7},{6,4},{7,9},{8,6},{9,11},{10,... | collective-permute-start | bytes 786440 | tf_op jit(solution)/shard_map/ppermute | solution.py:324
  54.1 7.7 %collective-permute-start.10 = (bf16[512,256]{1,0:T(8,128)(2,1)S(1)}, bf16[512,256]{1,0:T(8,128)(2,1)S(1)}, u32[]{:S(2)}, u32[]{:S(2)}) collective-permute-start(bf16[512,256]{1,0:T(8,128)(2,1)S(1)} %add_convert_fusion.2), channel_id=1, source_target_pairs={{0,14},{1,3},{2,0},{3,5},{4,2},{5,7},{6,4},{7,9},{8,6},{9,11},{10,... | collective-permute-start | bytes 786440 | tf_op jit(solution)/shard_map/ppermute | solution.py:324
  61.9 7.7 %collective-permute-start.11 = (bf16[512,256]{1,0:T(8,128)(2,1)S(1)}, bf16[512,256]{1,0:T(8,128)(2,1)S(1)}, u32[]{:S(2)}, u32[]{:S(2)}) collective-permute-start(bf16[512,256]{1,0:T(8,128)(2,1)S(1)} %add_convert_fusion.1), channel_id=1, source_target_pairs={{0,14},{1,3},{2,0},{3,5},{4,2},{5,7},{6,4},{7,9},{8,6},{9,11},{10,... | collective-permute-start | bytes 786440 | tf_op jit(solution)/shard_map/ppermute | solution.py:324
  69.0 2.7 %collective-permute-start.8 = (bf16[128,640]{1,0:T(8,128)(2,1)S(1)}, bf16[128,640]{1,0:T(8,128)(2,1)S(1)}, u32[]{:S(2)}, u32[]{:S(2)}) collective-permute-start(bf16[128,640]{1,0:T(8,128)(2,1)S(1)} %get-tuple-element.32), channel_id=1, source_target_pairs={{0,1},{1,0},{2,3},{3,2},{4,5},{5,4},{6,7},{7,6},{8,9},{9,8},{10,11... | collective-permute-start | bytes 491528 | tf_op jit(solution)/shard_map/ppermute | solution.py:328
  69.6 6.4 %collective-permute-start.12 = (bf16[256,256]{1,0:T(8,128)(2,1)S(1)}, bf16[256,256]{1,0:T(8,128)(2,1)S(1)}, u32[]{:S(2)}, u32[]{:S(2)}) collective-permute-start(bf16[256,256]{1,0:T(8,128)(2,1)S(1)} %get-tuple-element.50), channel_id=1, source_target_pairs={{0,0},{1,3},{2,2},{3,5},{4,4},{5,7},{6,6},{7,9},{8,8},{9,11},{10,1... | collective-permute-start | bytes 393224 | tf_op jit(solution)/shard_map/ppermute | solution.py:340
  70.3 7.9 %collective-permute-start.13 = (bf16[256,256]{1,0:T(8,128)(2,1)S(1)}, bf16[256,256]{1,0:T(8,128)(2,1)S(1)}, u32[]{:S(2)}, u32[]{:S(2)}) collective-permute-start(bf16[256,256]{1,0:T(8,128)(2,1)S(1)} %get-tuple-element.51), channel_id=1, source_target_pairs={{0,1},{1,2},{2,3},{3,4},{4,5},{5,6},{6,7},{7,8},{8,9},{9,10},{10,1... | collective-permute-start | bytes 393224 | tf_op jit(solution)/shard_map/ppermute | solution.py:341
  71.7 20.9 %copy-start.2 = (bf16[1024,128]{1,0:T(8,128)(2,1)S(1)}, bf16[1024,128]{1,0:T(8,128)(2,1)}, u32[]{:S(2)}) copy-start(bf16[1024,128]{1,0:T(8,128)(2,1)} %w_key.3) | copy-start | bytes 786436
  71.7 20.9 %copy-start.4 = (bf16[1024,128]{1,0:T(8,128)(2,1)S(1)}, bf16[1024,128]{1,0:T(8,128)(2,1)}, u32[]{:S(2)}) copy-start(bf16[1024,128]{1,0:T(8,128)(2,1)} %w_value.3) | copy-start | bytes 786436
  72.7 9.5 %collective-permute-start.19 = (bf16[512,256]{1,0:T(8,128)(2,1)S(1)}, bf16[512,256]{1,0:T(8,128)(2,1)S(1)}, u32[]{:S(2)}, u32[]{:S(2)}) collective-permute-start(bf16[512,256]{1,0:T(8,128)(2,1)S(1)} %get-tuple-element.45), channel_id=1, source_target_pairs={{0,64},{32,96},{64,128},{96,160},{128,192},{160,224},{192,0},{224,... | collective-permute-start | bytes 786440 | tf_op jit(solution)/shard_map/ppermute | solution.py:250
  73.6 10.8 %collective-permute-start.20 = (bf16[512,256]{1,0:T(8,128)(2,1)S(1)}, bf16[512,256]{1,0:T(8,128)(2,1)S(1)}, u32[]{:S(2)}, u32[]{:S(2)}) collective-permute-start(bf16[512,256]{1,0:T(8,128)(2,1)S(1)} %get-tuple-element.46), channel_id=1, source_target_pairs={{0,128},{32,160},{64,192},{96,224},{128,0},{160,32},{192,64},{224,... | collective-permute-start | bytes 786440 | tf_op jit(solution)/shard_map/ppermute | solution.py:250
  76.0 12.7 %collective-permute-start.21 = (bf16[512,256]{1,0:T(8,128)(2,1)S(1)}, bf16[512,256]{1,0:T(8,128)(2,1)S(1)}, u32[]{:S(2)}, u32[]{:S(2)}) collective-permute-start(bf16[512,256]{1,0:T(8,128)(2,1)S(1)} %get-tuple-element.47), channel_id=1, source_target_pairs={{0,192},{32,224},{64,0},{96,32},{128,64},{160,96},{192,128},{224,1... | collective-permute-start | bytes 786440 | tf_op jit(solution)/shard_map/ppermute | solution.py:250
  78.3 14.4 %collective-permute-start.14 = (bf16[128,256]{1,0:T(8,128)(2,1)S(1)}, bf16[128,256]{1,0:T(8,128)(2,1)S(1)}, u32[]{:S(2)}, u32[]{:S(2)}) collective-permute-start(bf16[128,256]{1,0:T(8,128)(2,1)S(1)} %slice.22), channel_id=1, source_target_pairs={{0,16},{1,17},{2,18},{3,19},{4,20},{5,21},{6,22},{7,23},{8,24},{9,... | collective-permute-start | bytes 196616 | tf_op jit(solution)/shard_map/ppermute | solution.py:343
  89.3 13.8 %collective-permute-start.22 = (bf16[512,128]{1,0:T(8,128)(2,1)S(1)}, bf16[512,128]{1,0:T(8,128)(2,1)S(1)}, u32[]{:S(2)}, u32[]{:S(2)}) collective-permute-start(bf16[512,128]{1,0:T(8,128)(2,1)S(1)} %get-tuple-element.49), channel_id=1, source_target_pairs={{0,32},{32,0},{64,96},{96,64},{128,160},{160,128},{192,224},{224,1... | collective-permute-start | bytes 393224 | tf_op jit(solution)/shard_map/ppermute | solution.py:258
  93.6 4.5 %collective-permute-start.15 = (bf16[128,256]{1,0:T(8,128)(2,1)S(1)}, bf16[128,256]{1,0:T(8,128)(2,1)S(1)}, u32[]{:S(2)}, u32[]{:S(2)}) collective-permute-start(bf16[128,256]{1,0:T(8,128)(2,1)S(1)} %get-tuple-element.39), channel_id=1, source_target_pairs={{0,64},{32,96},{64,128},{96,160},{128,192},{160,224},{192,0},{224,... | collective-permute-start | bytes 196616 | tf_op jit(solution)/shard_map/ppermute | solution.py:250
  94.6 6.4 %collective-permute-start.16 = (bf16[128,256]{1,0:T(8,128)(2,1)S(1)}, bf16[128,256]{1,0:T(8,128)(2,1)S(1)}, u32[]{:S(2)}, u32[]{:S(2)}) collective-permute-start(bf16[128,256]{1,0:T(8,128)(2,1)S(1)} %get-tuple-element.40), channel_id=1, source_target_pairs={{0,128},{32,160},{64,192},{96,224},{128,0},{160,32},{192,64},{224,... | collective-permute-start | bytes 196616 | tf_op jit(solution)/shard_map/ppermute | solution.py:250
  96.7 5.5 %collective-permute-start.17 = (bf16[128,256]{1,0:T(8,128)(2,1)S(1)}, bf16[128,256]{1,0:T(8,128)(2,1)S(1)}, u32[]{:S(2)}, u32[]{:S(2)}) collective-permute-start(bf16[128,256]{1,0:T(8,128)(2,1)S(1)} %get-tuple-element.41), channel_id=1, source_target_pairs={{0,192},{32,224},{64,0},{96,32},{128,64},{160,96},{192,128},{224,1... | collective-permute-start | bytes 196616 | tf_op jit(solution)/shard_map/ppermute | solution.py:250
  102.7 5.5 %collective-permute-start.18 = (bf16[128,128]{1,0:T(8,128)(2,1)S(1)}, bf16[128,128]{1,0:T(8,128)(2,1)S(1)}, u32[]{:S(2)}, u32[]{:S(2)}) collective-permute-start(bf16[128,128]{1,0:T(8,128)(2,1)S(1)} %get-tuple-element.43), channel_id=1, source_target_pairs={{0,32},{32,0},{64,96},{96,64},{128,160},{160,128},{192,224},{224,1... | collective-permute-start | bytes 98312 | tf_op jit(solution)/shard_map/ppermute | solution.py:258
  (1 other events, 0.9 us)
